TPU v7x, 32 devices: a whole 2x2x4 slice. The times are simulated.
32 devices in a mesh: gx: 16 (over z, x, core), gy: 2 (over y).
Axes of the slice: x: 2, y: 2, z: 4, core: 2. Of those that a mesh axis runs over, the one named last changes fastest.
Arguments:
- velocity: float32 [3, 32, 384, 128], P(None, 'gx', 'gy'), may hold values from -0.8 to 2.3
- stiffness: float32 [2], P('gy'), may hold values from 100 to 100000
- block_inverse: float32 [3, 384, 192], P(None, 'gy'), as said below
Outputs:
- velocity_next: float32 [3, 32, 384, 128], P(None, 'gx', 'gy')
Inputs may be any that keep to these rules, and one draw needn't show every extreme that they name: block_inverse[s] for block k is, to float32 rounding, the inverse of the 192-row matrix with 1 + 2 b on its diagonal and -b beside it, b = alpha_s stiffness[k].
All inputs are finite; a program needn't handle non-finite values.
Results may differ from a plain program's by a relative error of at most 0.0003.
Values sent between devices are 32-bit elements; how exact they have to be, the bound alone decides.
A program may use at most 64 MiB of HBM per device.

v0:
```python
import jax
import jax.numpy as jnp
from jax import lax
from jax.sharding import PartitionSpec as P

SUBSTEPS = 3


implicit_share = (8.0 / 15.0, 2.0 / 15.0, 1.0 / 3.0)
new_weight = (8.0 / 15.0, 5.0 / 12.0, 3.0 / 4.0)
old_weight = (0.0, -17.0 / 60.0, -5.0 / 12.0)
courant = (0.3, 0.2, 0.3)


def with_halo(cells, sides, width, closed):
    for axis, dim in sides:
        count = lax.axis_size(axis)
        ends = count if closed else count - 1
        head = lax.slice_in_dim(cells, 0, width, axis=dim)
        tail = lax.slice_in_dim(cells, cells.shape[dim] - width, cells.shape[dim], axis=dim)
        cells = jnp.concatenate(
            [
                lax.ppermute(tail, axis, [(i, (i + 1) % count) for i in range(ends)]),
                cells,
                lax.ppermute(head, axis, [((i + 1) % count, i) for i in range(ends)]),
            ],
            axis=dim,
        )
    return cells


def upwind(field, back_two, back_one, ahead_one, ahead_two, speed):
    behind = 1.5 * field - 2.0 * back_one + 0.5 * back_two
    ahead = -1.5 * field + 2.0 * ahead_one - 0.5 * ahead_two
    return jnp.maximum(speed, 0.0) * behind + jnp.minimum(speed, 0.0) * ahead


def reduced(first_vals, last_vals, tips):
    count = first_vals.shape[0]
    prev_q = jnp.zeros((), jnp.float32)
    prev_last = jnp.zeros_like(first_vals[0])
    fronts, backs, front_qs, back_qs = ([], [], [], [])
    for block in range(count):
        head_v = tips[0][block]
        tail_v = tips[1][block]
        head_w = tips[2][block]
        tail_w = tips[3][block]
        pivot = 1.0 - head_v * prev_q
        front = (first_vals[block] - head_v * prev_last) / pivot
        back = last_vals[block] - tail_v * prev_last + tail_v * prev_q * front
        front_q = head_w / pivot
        back_q = tail_w + tail_v * prev_q * front_q
        fronts.append(front)
        backs.append(back)
        front_qs.append(front_q)
        back_qs.append(back_q)
        prev_q = back_q
        prev_last = back
    heads = [None] * count
    tails = [None] * count
    heads[count - 1] = fronts[count - 1]
    tails[count - 1] = backs[count - 1]
    for block in range(count - 2, -1, -1):
        after = heads[block + 1]
        heads[block] = fronts[block] - front_qs[block] * after
        tails[block] = backs[block] - back_qs[block] * after
    zero = jnp.zeros_like(first_vals[0])
    lower_prev = jnp.stack([zero] + tails[:-1])
    upper_next = jnp.stack(heads[1:] + [zero])
    return (lower_prev, upper_next)


def body(velocity, stiffness, block_inverse):
    blocks = lax.axis_size("gy")
    own_index = lax.axis_index("gy")
    spans = velocity.shape[3]
    stiff = stiffness[0]
    first_flag = (own_index > 0).astype(jnp.float32)
    last_flag = (own_index < blocks - 1).astype(jnp.float32)
    coupling = -jnp.array(implicit_share, jnp.float32) * stiff
    lower = coupling * first_flag
    upper = coupling * last_flag
    column_v = block_inverse[:, :, 0] * lower[:, None]
    column_w = block_inverse[:, :, -1] * upper[:, None]
    own_tips = jnp.stack(
        [column_v[:, 0], column_v[:, -1], column_w[:, 0], column_w[:, -1]], axis=1
    )[:, :, None]
    every_tip = lax.all_gather(own_tips, "gy", axis=2, tiled=True)
    current = velocity
    previous = velocity
    for step in range(SUBSTEPS):
        widened = with_halo(current, (("gx", 1),), 2, True)
        middle = widened[:, 2:-2]
        ypadded = with_halo(middle, (("gy", 2),), 2, False)
        along_x = upwind(
            middle,
            widened[:, 0:-4],
            widened[:, 1:-3],
            widened[:, 3:-1],
            widened[:, 4:],
            middle[0:1],
        )
        along_y = upwind(
            middle,
            ypadded[:, :, 0:-4],
            ypadded[:, :, 1:-3],
            ypadded[:, :, 3:-1],
            ypadded[:, :, 4:],
            middle[1:2],
        )
        along_z = upwind(
            middle,
            jnp.roll(middle, 2, 3),
            jnp.roll(middle, 1, 3),
            jnp.roll(middle, -1, 3),
            jnp.roll(middle, -2, 3),
            middle[2:3],
        )
        advect = courant[0] * along_x + courant[1] * along_y + courant[2] * along_z
        diffuse = stiff * (ypadded[:, :, 3:-1] - 2.0 * middle + ypadded[:, :, 1:-3])
        forcing = middle + implicit_share[step] * diffuse - new_weight[step] * advect
        if step > 0:
            forcing = forcing - old_weight[step] * previous
        previous = advect
        planes = middle.shape[1]
        solved = jnp.einsum(
            "ij,cxjz->cxiz", block_inverse[step], forcing, precision=lax.Precision.HIGHEST
        )
        edges = jnp.stack([solved[:, :, 0, :], solved[:, :, -1, :]]).reshape(2, -1)
        tips = every_tip[step]
        whole = lax.all_gather(edges[:, None, :], "gy", axis=1, tiled=True)
        lower_prev, upper_next = reduced(whole[0], whole[1], tips)
        lower_own = lax.dynamic_slice_in_dim(lower_prev, own_index, 1, 0)[0]
        upper_own = lax.dynamic_slice_in_dim(upper_next, own_index, 1, 0)[0]
        lower_own = lower_own.reshape(3, planes, spans)[:, :, None, :]
        upper_own = upper_own.reshape(3, planes, spans)[:, :, None, :]
        current = (
            solved
            - column_v[step][None, None, :, None] * lower_own
            - column_w[step][None, None, :, None] * upper_own
        )
    return current


def solution(mesh):
    return jax.shard_map(
        body,
        mesh=mesh,
        in_specs=(P(None, "gx", "gy", None), P("gy"), P(None, "gy", None)),
        out_specs=P(None, "gx", "gy", None),
        check_vma=False,
    )
```

profile of v0, /device:TPU:1, one launch (start us, length us, event | category | flops | bytes accessed | tf_op | source)
XLA Modules:
  0.0 91.8 jit_solution(340637569167171038)
XLA Ops:
  0.0 2.6 %collective-permute-start.2 = (f32[3,2,192,128]{3,2,1,0:T(8,128)}, f32[3,2,192,128]{3,2,1,0:T(8,128)}, u32[]{:S(2)}, u32[]{:S(2)}) collective-permute-start(f32[3,2,192,128]{3,2,1,0:T(8,128)} %param.4), channel_id=1, source_target_pairs={{0,2},{2,4},{4,6},{6,8},{8,10},{10,12},{12,14},{14,16},{16,18},{18... | collective-permute-start | bytes 1769480 | tf_op jit(solution)/shard_map/ppermute | solution.py:23
  2.6 0.8 fusion.230
  3.4 1.3 %collective-permute-start = (f32[3,2,2,128]{3,2,1,0:T(2,128)S(1)}, f32[3,2,2,128]{3,2,1,0:T(2,128)S(1)}, u32[]{:S(2)}, u32[]{:S(2)}) collective-permute-start(f32[3,2,2,128]{3,2,1,0:T(2,128)S(1)} %get-tuple-element.66), channel_id=1, source_target_pairs={{1,0},{3,2},{5,4},{7,6},{9,8},{11,10},{13,12},{15,14},{17,16},{19,... | collective-permute-start | bytes 18440 | tf_op jit(solution)/shard_map/ppermute | solution.py:25
  4.7 4.0 %collective-permute-start.1 = (f32[3,2,2,128]{3,2,1,0:T(2,128)S(1)}, f32[3,2,2,128]{3,2,1,0:T(2,128)S(1)}, u32[]{:S(2)}, u32[]{:S(2)}) collective-permute-start(f32[3,2,2,128]{3,2,1,0:T(2,128)S(1)} %get-tuple-element.65), channel_id=1, source_target_pairs={{0,1},{2,3},{4,5},{6,7},{8,9},{10,11},{12,13},{14,15},{16,17},{18,... | collective-permute-start | bytes 18440 | tf_op jit(solution)/shard_map/ppermute | solution.py:23
  8.7 2.1 %maximum_bitcast_fusion.8 = (f32[2,192,128]{2,1,0:T(8,128)S(1)}, f32[2,192,128]{2,1,0:T(8,128)S(1)}, f32[2,192,128]{2,1,0:T(8,128)}, f32[2,192,128]{2,1,0:T(8,12...) fusion(f32[3,2,192,128]{3,2,1,0:T(8,128)} %param.4), kind=kLoop, calls=%fused_computation.229 | loop fusion | flops 294912 | bytes 1769472 | tf_op jit(solution)/shard_map/mul | solution.py:35
  10.8 0.2 fusion.226
  11.0 1.1 %fusion.227 = (f32[3,2,192,2]{3,2,1,0:T(8,128)S(1)}, f32[3,2,192,2]{3,2,1,0:T(8,128)}) fusion(f32[3,2,192,128]{3,2,1,0:T(8,128)S(1)} %copy-done), kind=kLoop, calls=%fused_computation.309 | loop fusion | bytes 36864 | tf_op jit(solution)/shard_map/jit(_roll_static)/slice | solution.py:116
  12.1 1.2 %fusion.228 = (f32[3,2,192,127]{3,2,1,0:T(8,128)}, f32[3,2,192,127]{3,2,1,0:T(8,128)}) fusion(f32[3,2,192,128]{3,2,1,0:T(8,128)S(1)} %copy-done), kind=kLoop, calls=%fused_computation.310 | loop fusion | bytes 2340864 | tf_op jit(solution)/shard_map/jit(_roll_static)/slice | solution.py:115
  13.9 1.4 %fusion.224 = (f32[3,192,1]{2,1,0:T(8,128)S(1)}, f32[3,192]{1,0:T(4,128)S(1)}) fusion(f32[3,192,192]{2,1,0:T(8,128)} %param.6), kind=kLoop, calls=%fused_computation.306 | loop fusion | bytes 9216 | tf_op jit(solution)/shard_map/slice | solution.py:83
  15.3 0.2 copy.17
  15.4 0.7 copy-done.2
  16.4 3.2 %all_gather.13 = f32[3,4,2]{1,0,2:T(4,128)S(1)} all-gather(f32[3,4,1]{1,0,2:T(4,128)S(1)} %maximum_bitcast_fusion.9), channel_id=1, replica_groups=mesh['gx'=16,'gy'=2] {'gy'}, dimensions={2}, use_global_device_ids=true | all-gather | bytes 144 | tf_op jit(solution)/shard_map/all_gather | solution.py:88
  19.6 1.2 %fusion.229 = (f32[3,2,192,1]{3,2,1,0:T(8,128)}, f32[3,2,192,1]{3,2,1,0:T(8,128)}) fusion(f32[3,2,192,128]{3,2,1,0:T(8,128)S(1)} %copy-done), kind=kLoop, calls=%fused_computation.311 | loop fusion | bytes 18432 | tf_op jit(solution)/shard_map/jit(_roll_static)/slice | solution.py:115
  20.8 0.7 fusion.233
  31.1 3.9 %fusion.61 = f32[3,2,192,128]{3,2,1,0:T(8,128)S(1)} fusion(f32[3,2,194,128]{3,2,1,0:T(8,128)S(1)} %constant_dynamic-update-slice_fusion, f32[3,2,192,128]{3,2,1,0:T(8,128)S(1)} %copy-done, f32[3,2,2,128]{3,2,1,0:T(2,128)S(1)} %collective-permute-done.1, f32[3,2,192,128]{3,2,1,0:T(8,128)} %collective-permute-done.3, ...), kind=kLoop, calls=%fused_computation.79 | loop fusion | flops 7077888 | bytes 7084032 | tf_op jit(solution)/shard_map/add | solution.py:119
  35.0 0.9 convolution_bitcast_fusion.2
  35.9 3.2 %all_gather.12 = f32[2,2,768]{2,0,1:T(2,128)S(1)} all-gather(f32[2,1,768]{2,0,1:T(2,128)S(1)} %pad_maximum_fusion.11), channel_id=1, replica_groups=mesh['gx'=16,'gy'=2] {'gy'}, dimensions={1}, use_global_device_ids=true | all-gather | bytes 18432 | tf_op jit(solution)/shard_map/all_gather | solution.py:131
  39.1 0.6 bitcast_subtract_fusion.2
  40.0 0.2 fusion.219
  40.3 0.2 fusion.220
  40.5 0.2 fusion.221
  40.7 4.7 %collective-permute-start.6 = (f32[3,2,192,128]{3,2,1,0:T(8,128)S(1)}, f32[3,2,192,128]{3,2,1,0:T(8,128)S(1)}, u32[]{:S(2)}, u32[]{:S(2)}) collective-permute-start(f32[3,2,192,128]{3,2,1,0:T(8,128)S(1)} %multiply_subtract_fusion.6), channel_id=1, source_target_pairs={{0,2},{2,4},{4,6},{6,8},{8,10},{10,12},{12,14},{14,16},{16,18},{18... | collective-permute-start | bytes 1769480 | tf_op jit(solution)/shard_map/ppermute | solution.py:23
  45.4 1.2 %collective-permute-start.7 = (f32[3,2,192,128]{3,2,1,0:T(8,128)S(1)}, f32[3,2,192,128]{3,2,1,0:T(8,128)S(1)}, u32[]{:S(2)}, u32[]{:S(2)}) collective-permute-start(f32[3,2,192,128]{3,2,1,0:T(8,128)S(1)} %multiply_subtract_fusion.6), channel_id=1, source_target_pairs={{2,0},{4,2},{6,4},{8,6},{10,8},{12,10},{14,12},{16,14},{18,16},{20... | collective-permute-start | bytes 1769480 | tf_op jit(solution)/shard_map/ppermute | solution.py:25
  46.6 1.3 %collective-permute-start.4 = (f32[3,2,2,128]{3,2,1,0:T(2,128)S(1)}, f32[3,2,2,128]{3,2,1,0:T(2,128)S(1)}, u32[]{:S(2)}, u32[]{:S(2)}) collective-permute-start(f32[3,2,2,128]{3,2,1,0:T(2,128)S(1)} %get-tuple-element.46), channel_id=1, source_target_pairs={{1,0},{3,2},{5,4},{7,6},{9,8},{11,10},{13,12},{15,14},{17,16},{19,... | collective-permute-start | bytes 18440 | tf_op jit(solution)/shard_map/ppermute | solution.py:25
  47.8 4.0 %collective-permute-start.5 = (f32[3,2,2,128]{3,2,1,0:T(2,128)S(1)}, f32[3,2,2,128]{3,2,1,0:T(2,128)S(1)}, u32[]{:S(2)}, u32[]{:S(2)}) collective-permute-start(f32[3,2,2,128]{3,2,1,0:T(2,128)S(1)} %get-tuple-element.45), channel_id=1, source_target_pairs={{0,1},{2,3},{4,5},{6,7},{8,9},{10,11},{12,13},{14,15},{16,17},{18,... | collective-permute-start | bytes 18440 | tf_op jit(solution)/shard_map/ppermute | solution.py:23
  51.8 0.2 fusion.222
  52.2 0.4 collective-permute-done.5
  52.6 5.9 %collective-permute-done.6 = f32[3,2,192,128]{3,2,1,0:T(8,128)S(1)} collective-permute-done((f32[3,2,192,128]{3,2,1,0:T(8,128)S(1)}, f32[3,2,192,128]{3,2,1,0:T(8,128)S(1)}, u32[]{:S(2)}, u32[]{:S(2)}) %collective-permute-start.6) | collective-permute-done | bytes 589856 | tf_op jit(solution)/shard_map/ppermute | solution.py:23
  58.5 2.5 %collective-permute-done.7 = f32[3,2,192,128]{3,2,1,0:T(8,128)S(1)} collective-permute-done((f32[3,2,192,128]{3,2,1,0:T(8,128)S(1)}, f32[3,2,192,128]{3,2,1,0:T(8,128)S(1)}, u32[]{:S(2)}, u32[]{:S(2)}) %collective-permute-start.7) | collective-permute-done | bytes 589856 | tf_op jit(solution)/shard_map/ppermute | solution.py:25
  61.0 1.4 %fusion.42 = f32[3,2,192,128]{3,2,1,0:T(8,128)S(1)} fusion(f32[3,2,2,128]{3,2,1,0:T(2,128)S(1)} %collective-permute-done.4, f32[3,2,192,128]{3,2,1,0:T(8,128)S(1)} %multiply_subtract_fusion.6, f32[3,2,2,128]{3,2,1,0:T(2,128)S(1)} %collective-permute-done.5, f32[3,2,192,128]{3,2,1,0:T(8,128)S(1)} %collective-permute-done.7, ...), kind=kLoop, calls=%fused_computation.56 | loop fusion | flops 7372800 | bytes 5910528 | tf_op jit(solution)/shard_map/add | solution.py:119
  62.3 1.0 %convolution_bitcast_fusion.1 = f32[3,2,192,128]{3,2,1,0:T(8,128)S(1)} fusion(f32[3,2,192,128]{3,2,1,0:T(8,128)S(1)} %fusion.61, f32[3,2,192,128]{3,2,1,0:T(8,128)S(1)} %fusion.42, f32[3,2,192,128]{3,2,1,0:T(8,128)S(1)} %multiply_subtract_fusion.6, f32[]{:T(128)} %bitcast.155, f32[3,192,192]{2,1,0:T(8,128)S(1)} %copy-done.1, ...), kind=kOutput, calls=%fused_computation.1 | convolution fusion | flops 341508096 | bytes 2568196 | tf_op jit(solution)/shard_map/ij,cxjz->cxiz/dot_general | solution.py:126
  63.3 3.2 %all_gather.14 = f32[2,2,768]{2,0,1:T(2,128)S(1)} all-gather(f32[2,1,768]{2,0,1:T(2,128)S(1)} %pad_maximum_fusion.12), channel_id=1, replica_groups=mesh['gx'=16,'gy'=2] {'gy'}, dimensions={1}, use_global_device_ids=true | all-gather | bytes 18432 | tf_op jit(solution)/shard_map/all_gather | solution.py:131
  66.6 0.7 bitcast_subtract_fusion.1
  67.3 0.2 multiply_subtract_fusion.5
  67.5 0.2 fusion.213
  67.7 0.2 fusion.214
  67.9 0.2 fusion.215
  68.1 1.2 %collective-permute-start.10 = (f32[3,2,192,128]{3,2,1,0:T(8,128)S(1)}, f32[3,2,192,128]{3,2,1,0:T(8,128)S(1)}, u32[]{:S(2)}, u32[]{:S(2)}) collective-permute-start(f32[3,2,192,128]{3,2,1,0:T(8,128)S(1)} %multiply_subtract_fusion.5), channel_id=1, source_target_pairs={{0,2},{2,4},{4,6},{6,8},{8,10},{10,12},{12,14},{14,16},{16,18},{18... | collective-permute-start | bytes 1769480 | tf_op jit(solution)/shard_map/ppermute | solution.py:23
  69.3 1.3 %collective-permute-start.8 = (f32[3,2,2,128]{3,2,1,0:T(2,128)S(1)}, f32[3,2,2,128]{3,2,1,0:T(2,128)S(1)}, u32[]{:S(2)}, u32[]{:S(2)}) collective-permute-start(f32[3,2,2,128]{3,2,1,0:T(2,128)S(1)} %get-tuple-element.28), channel_id=1, source_target_pairs={{1,0},{3,2},{5,4},{7,6},{9,8},{11,10},{13,12},{15,14},{17,16},{19,... | collective-permute-start | bytes 18440 | tf_op jit(solution)/shard_map/ppermute | solution.py:25
  70.6 4.0 %collective-permute-start.9 = (f32[3,2,2,128]{3,2,1,0:T(2,128)S(1)}, f32[3,2,2,128]{3,2,1,0:T(2,128)S(1)}, u32[]{:S(2)}, u32[]{:S(2)}) collective-permute-start(f32[3,2,2,128]{3,2,1,0:T(2,128)S(1)} %get-tuple-element.27), channel_id=1, source_target_pairs={{0,1},{2,3},{4,5},{6,7},{8,9},{10,11},{12,13},{14,15},{16,17},{18,... | collective-permute-start | bytes 18440 | tf_op jit(solution)/shard_map/ppermute | solution.py:23
  74.6 0.2 fusion.216
  75.0 0.4 collective-permute-done.9
  75.4 7.1 %collective-permute-done.10 = f32[3,2,192,128]{3,2,1,0:T(8,128)S(1)} collective-permute-done((f32[3,2,192,128]{3,2,1,0:T(8,128)S(1)}, f32[3,2,192,128]{3,2,1,0:T(8,128)S(1)}, u32[]{:S(2)}, u32[]{:S(2)}) %collective-permute-start.10) | collective-permute-done | bytes 589856 | tf_op jit(solution)/shard_map/ppermute | solution.py:23
  82.5 2.1 %collective-permute-done.11 = f32[3,2,192,128]{3,2,1,0:T(8,128)S(1)} collective-permute-done((f32[3,2,192,128]{3,2,1,0:T(8,128)S(1)}, f32[3,2,192,128]{3,2,1,0:T(8,128)S(1)}, u32[]{:S(2)}, u32[]{:S(2)}) %collective-permute-start.11) | collective-permute-done | bytes 589856 | tf_op jit(solution)/shard_map/ppermute | solution.py:25
  84.6 2.3 %convolution_bitcast_fusion = f32[3,2,192,128]{3,2,1,0:T(8,128)S(1)} fusion(f32[3,2,2,128]{3,2,1,0:T(2,128)S(1)} %collective-permute-done.8, f32[3,2,192,128]{3,2,1,0:T(8,128)S(1)} %multiply_subtract_fusion.5, f32[3,2,2,128]{3,2,1,0:T(2,128)S(1)} %collective-permute-done.9, f32[3,2,192,128]{3,2,1,0:T(8,128)S(1)} %collective-permute-done.11, ...), kind=kOutput, calls=%fused_computation | convolution fusion | flops 348585984 | bytes 9056260 | tf_op jit(solution)/shard_map/ij,cxjz->cxiz/dot_general | solution.py:126
  86.9 3.2 %all_gather.15 = f32[2,2,768]{2,0,1:T(2,128)S(1)} all-gather(f32[2,1,768]{2,0,1:T(2,128)S(1)} %pad_maximum_fusion.13), channel_id=1, replica_groups=mesh['gx'=16,'gy'=2] {'gy'}, dimensions={1}, use_global_device_ids=true | all-gather | bytes 18432 | tf_op jit(solution)/shard_map/all_gather | solution.py:131
  90.1 0.6 bitcast_subtract_fusion
  90.8 1.0 %multiply_subtract_fusion.4 = f32[3,2,192,128]{3,2,1,0:T(8,128)} fusion(f32[3,2,192,128]{3,2,1,0:T(8,128)S(1)} %convolution_bitcast_fusion, f32[3,2,128]{2,1,0:T(2,128)S(1)} %bitcast.157, f32[192]{0:T(256)S(1)} %bitcast.169, f32[3,2,128]{2,1,0:T(2,128)S(1)} %bitcast.156, f32[192]{0:T(256)S(1)} %bitcast.168), kind=kLoop, calls=%fused_computation.148 | loop fusion | flops 589824 | bytes 1187328 | tf_op jit(solution)/shard_map/sub | solution.py:138
  (39 shorter events, 1.0 us)
Async XLA Ops:
  0.0 31.1 %collective-permute-start.2 = (f32[3,2,192,128]{3,2,1,0:T(8,128)}, f32[3,2,192,128]{3,2,1,0:T(8,128)}, u32[]{:S(2)}, u32[]{:S(2)}) collective-permute-start(f32[3,2,192,128]{3,2,1,0:T(8,128)} %param.4), channel_id=1, source_target_pairs={{0,2},{2,4},{4,6},{6,8},{8,10},{10,12},{12,14},{14,16},{16,18},{18... | collective-permute-start | bytes 1769480 | tf_op jit(solution)/shard_map/ppermute | solution.py:23
  2.6 28.5 %collective-permute-start.3 = (f32[3,2,192,128]{3,2,1,0:T(8,128)}, f32[3,2,192,128]{3,2,1,0:T(8,128)}, u32[]{:S(2)}, u32[]{:S(2)}) collective-permute-start(f32[3,2,192,128]{3,2,1,0:T(8,128)} %param.4), channel_id=1, source_target_pairs={{2,0},{4,2},{6,4},{8,6},{10,8},{12,10},{14,12},{16,14},{18,16},{20... | collective-permute-start | bytes 1769480 | tf_op jit(solution)/shard_map/ppermute | solution.py:25
  3.4 27.6 %collective-permute-start = (f32[3,2,2,128]{3,2,1,0:T(2,128)S(1)}, f32[3,2,2,128]{3,2,1,0:T(2,128)S(1)}, u32[]{:S(2)}, u32[]{:S(2)}) collective-permute-start(f32[3,2,2,128]{3,2,1,0:T(2,128)S(1)} %get-tuple-element.66), channel_id=1, source_target_pairs={{1,0},{3,2},{5,4},{7,6},{9,8},{11,10},{13,12},{15,14},{17,16},{19,... | collective-permute-start | bytes 18440 | tf_op jit(solution)/shard_map/ppermute | solution.py:25
  4.7 26.4 %collective-permute-start.1 = (f32[3,2,2,128]{3,2,1,0:T(2,128)S(1)}, f32[3,2,2,128]{3,2,1,0:T(2,128)S(1)}, u32[]{:S(2)}, u32[]{:S(2)}) collective-permute-start(f32[3,2,2,128]{3,2,1,0:T(2,128)S(1)} %get-tuple-element.65), channel_id=1, source_target_pairs={{0,1},{2,3},{4,5},{6,7},{8,9},{10,11},{12,13},{14,15},{16,17},{18,... | collective-permute-start | bytes 18440 | tf_op jit(solution)/shard_map/ppermute | solution.py:23
  8.7 2.1 %copy-start = (f32[3,2,192,128]{3,2,1,0:T(8,128)S(1)}, f32[3,2,192,128]{3,2,1,0:T(8,128)}, u32[]{:S(2)}) copy-start(f32[3,2,192,128]{3,2,1,0:T(8,128)} %param.4) | copy-start | bytes 1769476
  15.4 0.7 copy-start.2
  31.1 3.9 %copy-start.1 = (f32[3,192,192]{2,1,0:T(8,128)S(1)}, f32[3,192,192]{2,1,0:T(8,128)}, u32[]{:S(2)}) copy-start(f32[3,192,192]{2,1,0:T(8,128)} %param.6) | copy-start | bytes 1327108
  40.7 17.8 %collective-permute-start.6 = (f32[3,2,192,128]{3,2,1,0:T(8,128)S(1)}, f32[3,2,192,128]{3,2,1,0:T(8,128)S(1)}, u32[]{:S(2)}, u32[]{:S(2)}) collective-permute-start(f32[3,2,192,128]{3,2,1,0:T(8,128)S(1)} %multiply_subtract_fusion.6), channel_id=1, source_target_pairs={{0,2},{2,4},{4,6},{6,8},{8,10},{10,12},{12,14},{14,16},{16,18},{18... | collective-permute-start | bytes 1769480 | tf_op jit(solution)/shard_map/ppermute | solution.py:23
  45.4 15.6 %collective-permute-start.7 = (f32[3,2,192,128]{3,2,1,0:T(8,128)S(1)}, f32[3,2,192,128]{3,2,1,0:T(8,128)S(1)}, u32[]{:S(2)}, u32[]{:S(2)}) collective-permute-start(f32[3,2,192,128]{3,2,1,0:T(8,128)S(1)} %multiply_subtract_fusion.6), channel_id=1, source_target_pairs={{2,0},{4,2},{6,4},{8,6},{10,8},{12,10},{14,12},{16,14},{18,16},{20... | collective-permute-start | bytes 1769480 | tf_op jit(solution)/shard_map/ppermute | solution.py:25
  46.6 5.6 %collective-permute-start.4 = (f32[3,2,2,128]{3,2,1,0:T(2,128)S(1)}, f32[3,2,2,128]{3,2,1,0:T(2,128)S(1)}, u32[]{:S(2)}, u32[]{:S(2)}) collective-permute-start(f32[3,2,2,128]{3,2,1,0:T(2,128)S(1)} %get-tuple-element.46), channel_id=1, source_target_pairs={{1,0},{3,2},{5,4},{7,6},{9,8},{11,10},{13,12},{15,14},{17,16},{19,... | collective-permute-start | bytes 18440 | tf_op jit(solution)/shard_map/ppermute | solution.py:25
  47.8 4.7 %collective-permute-start.5 = (f32[3,2,2,128]{3,2,1,0:T(2,128)S(1)}, f32[3,2,2,128]{3,2,1,0:T(2,128)S(1)}, u32[]{:S(2)}, u32[]{:S(2)}) collective-permute-start(f32[3,2,2,128]{3,2,1,0:T(2,128)S(1)} %get-tuple-element.45), channel_id=1, source_target_pairs={{0,1},{2,3},{4,5},{6,7},{8,9},{10,11},{12,13},{14,15},{16,17},{18,... | collective-permute-start | bytes 18440 | tf_op jit(solution)/shard_map/ppermute | solution.py:23
  68.1 14.4 %collective-permute-start.10 = (f32[3,2,192,128]{3,2,1,0:T(8,128)S(1)}, f32[3,2,192,128]{3,2,1,0:T(8,128)S(1)}, u32[]{:S(2)}, u32[]{:S(2)}) collective-permute-start(f32[3,2,192,128]{3,2,1,0:T(8,128)S(1)} %multiply_subtract_fusion.5), channel_id=1, source_target_pairs={{0,2},{2,4},{4,6},{6,8},{8,10},{10,12},{12,14},{14,16},{16,18},{18... | collective-permute-start | bytes 1769480 | tf_op jit(solution)/shard_map/ppermute | solution.py:23
  69.3 15.2 %collective-permute-start.11 = (f32[3,2,192,128]{3,2,1,0:T(8,128)S(1)}, f32[3,2,192,128]{3,2,1,0:T(8,128)S(1)}, u32[]{:S(2)}, u32[]{:S(2)}) collective-permute-start(f32[3,2,192,128]{3,2,1,0:T(8,128)S(1)} %multiply_subtract_fusion.5), channel_id=1, source_target_pairs={{2,0},{4,2},{6,4},{8,6},{10,8},{12,10},{14,12},{16,14},{18,16},{20... | collective-permute-start | bytes 1769480 | tf_op jit(solution)/shard_map/ppermute | solution.py:25
  69.3 5.6 %collective-permute-start.8 = (f32[3,2,2,128]{3,2,1,0:T(2,128)S(1)}, f32[3,2,2,128]{3,2,1,0:T(2,128)S(1)}, u32[]{:S(2)}, u32[]{:S(2)}) collective-permute-start(f32[3,2,2,128]{3,2,1,0:T(2,128)S(1)} %get-tuple-element.28), channel_id=1, source_target_pairs={{1,0},{3,2},{5,4},{7,6},{9,8},{11,10},{13,12},{15,14},{17,16},{19,... | collective-permute-start | bytes 18440 | tf_op jit(solution)/shard_map/ppermute | solution.py:25
  70.6 4.7 %collective-permute-start.9 = (f32[3,2,2,128]{3,2,1,0:T(2,128)S(1)}, f32[3,2,2,128]{3,2,1,0:T(2,128)S(1)}, u32[]{:S(2)}, u32[]{:S(2)}) collective-permute-start(f32[3,2,2,128]{3,2,1,0:T(2,128)S(1)} %get-tuple-element.27), channel_id=1, source_target_pairs={{0,1},{2,3},{4,5},{6,7},{8,9},{10,11},{12,13},{14,15},{16,17},{18,... | collective-permute-start | bytes 18440 | tf_op jit(solution)/shard_map/ppermute | solution.py:23
where the time goes:
time: 92.4 us; the launch traced here: 91.8 us
  starting transfers between devices  25.5 us (28%)
  waiting for transfers between devices  18.4 us (20%)
  blocking collectives  12.8 us (14%)
  other arithmetic  11 us (12%)
  between operations  10.5 us (11%)
  local copies, waits for them, and re-layouts  9.46 us (10%)
  matrix products  4.16 us (5%)
    ppermute x6, starting transfers between devices, with_halo(): lax.ppermute(tail, axis, [(i, (i + 1) % count) for i in range(ends)])  20.4 us
    ppermute x6, waiting for transfers between devices, with_halo(): lax.ppermute(tail, axis, [(i, (i + 1) % count) for i in range(ends)])  13.8 us
    all_gather x3, blocking collectives, body(): whole = lax.all_gather(edges[:, None, :], 'gy', axis=1, tiled=True)  9.64 us
    add x2, other arithmetic, body(): advect = courant[0] * along_x + courant[1] * along_y + courant[2] * along_z  5.22 us
    ppermute x6, starting transfers between devices, with_halo(): lax.ppermute(head, axis, [((i + 1) % count, i) for i in range(ends)])  5.05 us
    ppermute x6, waiting for transfers between devices, with_halo(): lax.ppermute(head, axis, [((i + 1) % count, i) for i in range(ends)])  4.59 us
    dot_general x3, matrix products, body(): jnp.einsum('ij,cxjz->cxiz', block_inverse[step], forcing, precision=lax.P...  4.16 us
    slice x6, local copies, waits for them, and re-layouts, body(): jnp.roll(middle, -1, 3)  3.27 us
  transfers between devices with their start and end apart: 12, of which 6 were waited for; matrix products, arithmetic and copies ran while one was open for 11% of the time, Pallas kernels for 0%

commit v1 on v0

v1 whole, which is shorter than its diff:
```python
import functools

import jax
import jax.numpy as jnp
from jax import lax
from jax.experimental import pallas as pl
from jax.experimental.pallas import tpu as pltpu
from jax.sharding import PartitionSpec as P

SUBSTEPS = 3
PAD = 8
MESH = pl.DeviceIdType.MESH

implicit_share = (8.0 / 15.0, 2.0 / 15.0, 1.0 / 3.0)
new_weight = (8.0 / 15.0, 5.0 / 12.0, 3.0 / 4.0)
old_weight = (0.0, -17.0 / 60.0, -5.0 / 12.0)
courant = (0.3, 0.2, 0.3)


def eliminate(edges, tips, planes, own):
    count = len(edges)
    zero = jnp.zeros_like(edges[0][0:planes])
    row = lambda b, r: edges[b][r * planes : (r + 1) * planes]
    v = lambda b, r: tips[b][r : r + 1]
    w = lambda b, r: tips[b][4 + r : 5 + r]
    prev_q, prev_last = jnp.zeros_like(tips[0][0:1]), zero
    fronts, backs, front_qs, back_qs = [], [], [], []
    for b in range(count):
        pivot = 1.0 - v(b, 0) * prev_q
        front = (row(b, 0) - v(b, 0) * prev_last) / pivot
        back = row(b, 3) - v(b, 3) * prev_last + v(b, 3) * prev_q * front
        front_q = w(b, 0) / pivot
        back_q = w(b, 3) + v(b, 3) * prev_q * front_q
        fronts.append(front)
        backs.append(back)
        front_qs.append(front_q)
        back_qs.append(back_q)
        prev_q, prev_last = back_q, back
    heads, tails = [None] * count, [None] * count
    heads[-1], tails[-1] = fronts[-1], backs[-1]
    for b in range(count - 2, -1, -1):
        heads[b] = fronts[b] - front_qs[b] * heads[b + 1]
        tails[b] = backs[b] - back_qs[b] * heads[b + 1]
    before = [zero] + tails[:-1]
    after = heads[1:] + [zero]

    def solved(b, r):
        return row(b, r) - v(b, r) * before[b] - w(b, r) * after[b]

    def pick(values):
        out = values[0]
        for b in range(1, count):
            out = jnp.where(own == b, values[b], out)
        return out

    above = [pick([zero] + [solved(b, r) for b in range(count - 1)]) for r in (2, 3)]
    below = [pick([solved(b, r) for b in range(1, count)] + [zero]) for r in (0, 1)]
    return pick(before), pick(after), above, below


def kernel(
    n_x,
    n_y,
    stiff_ref,
    vel_ref,
    inv_ref,
    out_ref,
    u_ref,
    left_ref,
    right_ref,
    prev_ref,
    rhs_ref,
    g_ref,
    v_ref,
    w_ref,
    raw_ref,
    edge_ref,
    tip_ref,
    x_send,
    x_recv,
    raw_send,
    raw_recv,
    edge_send,
    edge_recv,
    tip_send,
    tip_recv,
):
    comps, planes, rows, lanes = vel_ref.shape
    me_x, me_y = lax.axis_index("gx"), lax.axis_index("gy")
    right, left = lax.rem(me_x + 1, n_x), lax.rem(me_x + n_x - 1, n_x)
    others = [lax.rem(me_y + off, n_y) for off in range(1, n_y)]
    chunk = 32 if rows % 32 == 0 else 8
    chunks = rows // chunk

    barrier = pltpu.get_barrier_semaphore()
    for side in (left, right):
        pl.semaphore_signal(barrier, inc=1, device_id={"gx": side}, device_id_type=MESH)
    for other in others:
        pl.semaphore_signal(barrier, inc=1, device_id={"gy": other}, device_id_type=MESH)
    pl.semaphore_wait(barrier, 2 + len(others))

    def x_copies(step, c):
        if step == 0:
            tail, head = vel_ref.at[c, planes - 2 : planes], vel_ref.at[c, 0:2]
        else:
            tail = u_ref.at[step, c, planes - 2 : planes, PAD : PAD + rows]
            head = u_ref.at[step, c, 0:2, PAD : PAD + rows]
        return [
            pltpu.make_async_remote_copy(
                tail, left_ref.at[step, c], x_send.at[step, c, 0], x_recv.at[step, c, 0],
                device_id={"gx": right}, device_id_type=MESH,
            ),
            pltpu.make_async_remote_copy(
                head, right_ref.at[step, c], x_send.at[step, c, 1], x_recv.at[step, c, 1],
                device_id={"gx": left}, device_id_type=MESH,
            ),
        ]

    def y_copies(ref, send, recv):
        return [
            pltpu.make_async_remote_copy(
                ref.at[me_y], ref.at[me_y], send.at[i], recv.at[i],
                device_id={"gy": other}, device_id_type=MESH,
            )
            for i, other in enumerate(others)
        ]

    def edge_copies(step, c):
        return y_copies(edge_ref.at[step, c], edge_send.at[step, c], edge_recv.at[step, c])

    for c in range(comps):
        for copy in x_copies(0, c):
            copy.start()
    for c in range(comps):
        for i, at in enumerate((0, 1, rows - 2, rows - 1)):
            for p in range(planes):
                raw_ref[me_y, c, i * planes + p : i * planes + p + 1, :] = vel_ref[c, p, at : at + 1, :]
    raw_copies = y_copies(raw_ref, raw_send, raw_recv)
    for copy in raw_copies:
        copy.start()
    stiff = stiff_ref[0]
    lower_flag = jnp.where(me_y > 0, 1.0, 0.0)
    upper_flag = jnp.where(me_y < n_y - 1, 1.0, 0.0)
    for s in range(SUBSTEPS):
        coupling = -implicit_share[s] * stiff
        column_v = inv_ref[s, :, 0:1] * (coupling * lower_flag)
        column_w = inv_ref[s, :, rows - 1 : rows] * (coupling * upper_flag)
        v_ref[s] = jnp.broadcast_to(column_v, (rows, lanes))
        w_ref[s] = jnp.broadcast_to(column_w, (rows, lanes))
        for i, at in enumerate((0, 1, rows - 2, rows - 1)):
            tip_ref[me_y, s, i : i + 1, :] = v_ref[s, at : at + 1, :]
            tip_ref[me_y, s, 4 + i : 5 + i, :] = w_ref[s, at : at + 1, :]
    tip_copies = y_copies(tip_ref, tip_send, tip_recv)
    for copy in tip_copies:
        copy.start()
    for c in range(comps):
        for p in range(planes):
            u_ref[0, c, p, PAD : PAD + rows, :] = vel_ref[c, p]

    def store_halo(step, c, above, below):
        for p in range(planes):
            for i in range(2):
                u_ref[step, c, p, PAD - 2 + i : PAD - 1 + i, :] = above[i][p : p + 1]
                u_ref[step, c, p, PAD + rows + i : PAD + rows + 1 + i, :] = below[i][p : p + 1]

    for copy in raw_copies:
        copy.wait()
    for c in range(comps):
        zero = jnp.zeros((planes, lanes), jnp.float32)
        above, below = [zero, zero], [zero, zero]
        for b in range(n_y):
            tile = raw_ref[b, c]
            for i in range(2):
                first = tile[i * planes : (i + 1) * planes]
                last = tile[(2 + i) * planes : (3 + i) * planes]
                above[i] = jnp.where(me_y == b + 1, last, above[i])
                below[i] = jnp.where(me_y == b - 1, first, below[i])
        store_halo(0, c, above, below)
    for copy in tip_copies:
        copy.wait()

    def force(step, c):
        copies = x_copies(step, c)
        for copy in copies:
            copy.wait_recv()

        @pl.loop(0, chunks)
        def _(k):
            base = pl.multiple_of(k * chunk, chunk)
            inner = pl.ds(base, chunk)
            own = pl.ds(pl.multiple_of(base + PAD, 8), chunk)
            for p in range(planes):
                def plane(i):
                    if i < 0:
                        return left_ref[step, c, 2 + i, inner, :]
                    if i >= planes:
                        return right_ref[step, c, i - planes, inner, :]
                    return u_ref[step, c, i, own, :]

                speed = [u_ref[step, d, p, own, :] for d in range(comps)]
                weight = [(0.5 * courant[d]) * jnp.abs(speed[d]) for d in range(comps)]
                window = u_ref[step, c, p, pl.ds(base, chunk + 2 * PAD), :]
                at = lambda i: window[PAD + i : PAD + i + chunk]
                field = at(0)
                y1, y_1 = at(1), at(-1)
                turn = lambda i: pltpu.roll(field, i % lanes, 1)
                total = 3.0 * field * (weight[0] + weight[1] + weight[2])
                for d, (m2, m1, p1, p2) in enumerate(
                    (
                        (plane(p - 2), plane(p - 1), plane(p + 1), plane(p + 2)),
                        (at(-2), y_1, y1, at(2)),
                        (turn(2), turn(1), turn(-1), turn(-2)),
                    )
                ):
                    up = speed[d] > 0.0
                    total = total + weight[d] * (
                        jnp.where(up, m2, p2) - 4.0 * jnp.where(up, m1, p1)
                    )
                diffuse = stiff * (y1 - 2.0 * field + y_1)
                forcing = field + implicit_share[step] * diffuse - new_weight[step] * total
                if step > 0:
                    forcing = forcing - old_weight[step] * prev_ref[c, p, inner, :]
                if step < SUBSTEPS - 1:
                    prev_ref[c, p, inner, :] = total
                rhs_ref[c, inner, p * lanes : (p + 1) * lanes] = forcing

        g_ref[c] = jnp.dot(
            inv_ref[step], rhs_ref[c],
            precision=lax.Precision.HIGHEST, preferred_element_type=jnp.float32,
        )
        for i, at in enumerate((0, 1, rows - 2, rows - 1)):
            for p in range(planes):
                edge_ref[step, c, me_y, i * planes + p : i * planes + p + 1, :] = g_ref[
                    c, at : at + 1, p * lanes : (p + 1) * lanes
                ]
        for copy in edge_copies(step, c):
            copy.start()

    def finish(step, c):
        for copy in edge_copies(step, c):
            copy.wait_recv()
        before, after, above, below = eliminate(
            [edge_ref[step, c, b] for b in range(n_y)],
            [tip_ref[b, step] for b in range(n_y)],
            planes,
            me_y,
        )

        @pl.loop(0, chunks)
        def _(k):
            base = pl.multiple_of(k * chunk, chunk)
            inner = pl.ds(base, chunk)
            own = pl.ds(pl.multiple_of(base + PAD, 8), chunk)
            for p in range(planes):
                fresh = (
                    g_ref[c, inner, p * lanes : (p + 1) * lanes]
                    - v_ref[step, inner, :] * before[p : p + 1]
                    - w_ref[step, inner, :] * after[p : p + 1]
                )
                if step < SUBSTEPS - 1:
                    u_ref[step + 1, c, p, own, :] = fresh
                else:
                    out_ref[c, p, inner, :] = fresh

        if step < SUBSTEPS - 1:
            for copy in x_copies(step + 1, c):
                copy.start()
            store_halo(step + 1, c, above, below)

    for step in range(SUBSTEPS):
        for c in range(comps):
            force(step, c)
            if c > 0:
                finish(step, c - 1)
        finish(step, comps - 1)

    for step in range(SUBSTEPS):
        for c in range(comps):
            for copy in x_copies(step, c) + edge_copies(step, c):
                copy.wait_send()


def body(n_x, n_y, velocity, stiffness, block_inverse):
    comps, planes, rows, lanes = velocity.shape
    tile = 4 * planes
    links = n_y - 1
    vmem = lambda *shape: pltpu.VMEM(shape, jnp.float32)
    return pl.pallas_call(
        functools.partial(kernel, n_x, n_y),
        out_shape=jax.ShapeDtypeStruct(velocity.shape, jnp.float32),
        in_specs=[
            pl.BlockSpec(memory_space=pltpu.SMEM),
            pl.BlockSpec(memory_space=pltpu.VMEM),
            pl.BlockSpec(memory_space=pltpu.VMEM),
        ],
        out_specs=pl.BlockSpec(memory_space=pltpu.VMEM),
        scratch_shapes=[
            vmem(SUBSTEPS, comps, planes, rows + 2 * PAD, lanes),
            vmem(SUBSTEPS, comps, 2, rows, lanes),
            vmem(SUBSTEPS, comps, 2, rows, lanes),
            vmem(comps, planes, rows, lanes),
            vmem(comps, rows, planes * lanes),
            vmem(comps, rows, planes * lanes),
            vmem(SUBSTEPS, rows, lanes),
            vmem(SUBSTEPS, rows, lanes),
            vmem(n_y, comps, tile, lanes),
            vmem(SUBSTEPS, comps, n_y, tile, lanes),
            vmem(n_y, SUBSTEPS, 8, lanes),
            pltpu.SemaphoreType.DMA((SUBSTEPS, comps, 2)),
            pltpu.SemaphoreType.DMA((SUBSTEPS, comps, 2)),
            pltpu.SemaphoreType.DMA((links,)),
            pltpu.SemaphoreType.DMA((links,)),
            pltpu.SemaphoreType.DMA((SUBSTEPS, comps, links)),
            pltpu.SemaphoreType.DMA((SUBSTEPS, comps, links)),
            pltpu.SemaphoreType.DMA((links,)),
            pltpu.SemaphoreType.DMA((links,)),
        ],
        compiler_params=pltpu.CompilerParams(
            collective_id=0, has_side_effects=True, vmem_limit_bytes=40 * 1024 * 1024
        ),
    )(stiffness, velocity, block_inverse)


def solution(mesh):
    return jax.shard_map(
        functools.partial(body, mesh.shape["gx"], mesh.shape["gy"]),
        mesh=mesh,
        in_specs=(P(None, "gx", "gy", None), P("gy"), P(None, "gy", None)),
        out_specs=P(None, "gx", "gy", None),
        check_vma=False,
    )
```

time: 92.4 us -> 53.4 us (0.58)
  Pallas kernels: 0 us -> 49.6 us
  starting transfers between devices: 25.5 us -> 0 us
  waiting for transfers between devices: 18.4 us -> 0 us
  blocking collectives: 12.8 us -> 0 us
  other arithmetic: 11 us -> 0 us
  between operations: 10.5 us -> 0.67 us
  local copies, waits for them, and re-layouts: 9.46 us -> 2.94 us
  matrix products: 4.16 us -> 0 us
    pallas_call x0 -> x1, Pallas kernels: none -> 49.6 us  [body(): pl.pallas_call(functools.partial(kernel, n_x, n_y), out_shape=jax.ShapeDt...]
    ppermute x12 -> x0, starting transfers between devices: 25.5 us -> none  [the longest x6 20.4 us: with_halo(): lax.ppermute(tail, axis, [(i, (i + 1) % count) for i in range(ends)])]
    ppermute x12 -> x0, waiting for transfers between devices: 18.4 us -> none  [the longest x6 13.8 us: with_halo(): lax.ppermute(tail, axis, [(i, (i + 1) % count) for i in range(ends)])]
    all_gather x4 -> x0, blocking collectives: 12.8 us -> none  [the longest x3 9.64 us: body(): whole = lax.all_gather(edges[:, None, :], 'gy', axis=1, tiled=True)]
    slice x24 -> x0, local copies, waits for them, and re-layouts: 8.44 us -> none  [the longest x6 3.27 us: body(): jnp.roll(middle, -1, 3)]
    add x2 -> x0, other arithmetic: 5.22 us -> none  [body(): advect = courant[0] * along_x + courant[1] * along_y + courant[2] * along_z]
    dot_general x3 -> x0, matrix products: 4.16 us -> none  [body(): jnp.einsum('ij,cxjz->cxiz', block_inverse[step], forcing, precision=lax.P...]
    sub x6 -> x0, other arithmetic: 3.3 us -> none  [the longest x3 1.94 us: reduced(): tails[block] = backs[block] - back_qs[block] * after]
  transfers between devices with their start and end apart: 12 -> 0, of which waited for: 6 -> 0; matrix products, arithmetic and copies ran while one was open for 11% -> 0% of each run, Pallas kernels for 0% -> 0%
where the time goes in v1:
time: 53.4 us; the launch traced here: 53.2 us
  Pallas kernels  49.6 us (93%)
  local copies, waits for them, and re-layouts  2.94 us (6%)
  between operations  0.67 us (1%)
    pallas_call x1, Pallas kernels, body(): pl.pallas_call(functools.partial(kernel, n_x, n_y), out_shape=jax.ShapeDt...  49.6 us
    unnamed x5, local copies, waits for them, and re-layouts  2.94 us

profile of v1, /device:TPU:1, one launch (start us, length us, event | category | flops | bytes accessed | tf_op | source)
XLA Modules:
  0.0 53.2 jit_solution(2236799751236973141)
XLA Ops:
  0.7 0.0 copy-start
  0.7 1.1 %copy-done = f32[3,2,192,128]{3,2,1,0:T(8,128)S(1)} copy-done((f32[3,2,192,128]{3,2,1,0:T(8,128)S(1)}, f32[3,2,192,128]{3,2,1,0:T(8,128)}, u32[]{:S(2)}) %copy-start) | copy-done | bytes 589848
  1.7 0.0 copy-start.1
  1.7 1.1 %copy-done.1 = f32[3,192,192]{2,1,0:T(8,128)S(1)} copy-done((f32[3,192,192]{2,1,0:T(8,128)S(1)}, f32[3,192,192]{2,1,0:T(8,128)}, u32[]{:S(2)}) %copy-start.1) | copy-done | bytes 442392
  2.8 49.6 %shard_map.37 = f32[3,2,192,128]{3,2,1,0:T(8,128)S(1)} custom-call(f32[1]{0:T(128)S(6)} %copy.5.stiff_ref, f32[3,2,192,128]{3,2,1,0:T(8,128)S(1)} %copy-done, f32[3,192,192]{2,1,0:T(8,128)S(1)} %copy-done.1), custom_call_target="tpu_custom_call" | custom-call | tf_op jit(solution)/shard_map/pallas_call | solution.py:288
  52.4 0.8 %copy.6 = f32[3,2,192,128]{3,2,1,0:T(8,128)} copy(f32[3,2,192,128]{3,2,1,0:T(8,128)S(1)} %shard_map.37) | data formatting | bytes 1179648
Async XLA Ops:
  0.7 1.1 %copy-start = (f32[3,2,192,128]{3,2,1,0:T(8,128)S(1)}, f32[3,2,192,128]{3,2,1,0:T(8,128)}, u32[]{:S(2)}) copy-start(f32[3,2,192,128]{3,2,1,0:T(8,128)} %vel_ref.1) | copy-start | bytes 1769476
  1.7 1.1 %copy-start.1 = (f32[3,192,192]{2,1,0:T(8,128)S(1)}, f32[3,192,192]{2,1,0:T(8,128)}, u32[]{:S(2)}) copy-start(f32[3,192,192]{2,1,0:T(8,128)} %inv_ref.1) | copy-start | bytes 1327108

commit v2 on v1

--- a/solution.py
+++ b/solution.py
@@ -63,8 +63,9 @@
     n_y,
     stiff_ref,
     vel_ref,
+    inv_hbm,
+    out_ref,
     inv_ref,
-    out_ref,
     u_ref,
     left_ref,
     right_ref,
@@ -84,14 +85,21 @@
     edge_recv,
     tip_send,
     tip_recv,
+    local_sem,
 ):
     comps, planes, rows, lanes = vel_ref.shape
     me_x, me_y = lax.axis_index("gx"), lax.axis_index("gy")
     right, left = lax.rem(me_x + 1, n_x), lax.rem(me_x + n_x - 1, n_x)
     others = [lax.rem(me_y + off, n_y) for off in range(1, n_y)]
-    chunk = 32 if rows % 32 == 0 else 8
+    chunk = next(size for size in (64, 32, 16, 8) if rows % size == 0)
     chunks = rows // chunk
 
+    own_copy = pltpu.make_async_copy(
+        vel_ref, u_ref.at[0, :, :, PAD : PAD + rows], local_sem.at[0]
+    )
+    inv_copy = pltpu.make_async_copy(inv_hbm, inv_ref, local_sem.at[1])
+    own_copy.start()
+    inv_copy.start()
     barrier = pltpu.get_barrier_semaphore()
     for side in (left, right):
         pl.semaphore_signal(barrier, inc=1, device_id={"gx": side}, device_id_type=MESH)
@@ -131,13 +139,17 @@
     for c in range(comps):
         for copy in x_copies(0, c):
             copy.start()
+    own_copy.wait()
     for c in range(comps):
         for i, at in enumerate((0, 1, rows - 2, rows - 1)):
             for p in range(planes):
-                raw_ref[me_y, c, i * planes + p : i * planes + p + 1, :] = vel_ref[c, p, at : at + 1, :]
+                raw_ref[me_y, c, i * planes + p : i * planes + p + 1, :] = u_ref[
+                    0, c, p, PAD + at : PAD + at + 1, :
+                ]
     raw_copies = y_copies(raw_ref, raw_send, raw_recv)
     for copy in raw_copies:
         copy.start()
+    inv_copy.wait()
     stiff = stiff_ref[0]
     lower_flag = jnp.where(me_y > 0, 1.0, 0.0)
     upper_flag = jnp.where(me_y < n_y - 1, 1.0, 0.0)
@@ -153,9 +165,6 @@
     tip_copies = y_copies(tip_ref, tip_send, tip_recv)
     for copy in tip_copies:
         copy.start()
-    for c in range(comps):
-        for p in range(planes):
-            u_ref[0, c, p, PAD : PAD + rows, :] = vel_ref[c, p]
 
     def store_halo(step, c, above, below):
         for p in range(planes):
@@ -179,24 +188,13 @@
     for copy in tip_copies:
         copy.wait()
 
-    def force(step, c):
-        copies = x_copies(step, c)
-        for copy in copies:
-            copy.wait_recv()
-
+    def prepare(step, c):
         @pl.loop(0, chunks)
         def _(k):
             base = pl.multiple_of(k * chunk, chunk)
             inner = pl.ds(base, chunk)
             own = pl.ds(pl.multiple_of(base + PAD, 8), chunk)
             for p in range(planes):
-                def plane(i):
-                    if i < 0:
-                        return left_ref[step, c, 2 + i, inner, :]
-                    if i >= planes:
-                        return right_ref[step, c, i - planes, inner, :]
-                    return u_ref[step, c, i, own, :]
-
                 speed = [u_ref[step, d, p, own, :] for d in range(comps)]
                 weight = [(0.5 * courant[d]) * jnp.abs(speed[d]) for d in range(comps)]
                 window = u_ref[step, c, p, pl.ds(base, chunk + 2 * PAD), :]
@@ -205,12 +203,9 @@
                 y1, y_1 = at(1), at(-1)
                 turn = lambda i: pltpu.roll(field, i % lanes, 1)
                 total = 3.0 * field * (weight[0] + weight[1] + weight[2])
-                for d, (m2, m1, p1, p2) in enumerate(
-                    (
-                        (plane(p - 2), plane(p - 1), plane(p + 1), plane(p + 2)),
-                        (at(-2), y_1, y1, at(2)),
-                        (turn(2), turn(1), turn(-1), turn(-2)),
-                    )
+                for d, (m2, m1, p1, p2) in (
+                    (1, (at(-2), y_1, y1, at(2))),
+                    (2, (turn(2), turn(1), turn(-1), turn(-2))),
                 ):
                     up = speed[d] > 0.0
                     total = total + weight[d] * (
@@ -224,6 +219,34 @@
                     prev_ref[c, p, inner, :] = total
                 rhs_ref[c, inner, p * lanes : (p + 1) * lanes] = forcing
 
+    def force(step, c):
+        for copy in x_copies(step, c):
+            copy.wait_recv()
+
+        @pl.loop(0, chunks)
+        def _(k):
+            base = pl.multiple_of(k * chunk, chunk)
+            inner = pl.ds(base, chunk)
+            own = pl.ds(pl.multiple_of(base + PAD, 8), chunk)
+            for p in range(planes):
+
+                def plane(i):
+                    if i < 0:
+                        return left_ref[step, c, 2 + i, inner, :]
+                    if i >= planes:
+                        return right_ref[step, c, i - planes, inner, :]
+                    return u_ref[step, c, i, own, :]
+
+                speed = u_ref[step, 0, p, own, :]
+                up = speed > 0.0
+                along = (0.5 * courant[0]) * jnp.abs(speed) * (
+                    jnp.where(up, plane(p - 2), plane(p + 2))
+                    - 4.0 * jnp.where(up, plane(p - 1), plane(p + 1))
+                )
+                if step < SUBSTEPS - 1:
+                    prev_ref[c, p, inner, :] += along
+                rhs_ref[c, inner, p * lanes : (p + 1) * lanes] -= new_weight[step] * along
+
         g_ref[c] = jnp.dot(
             inv_ref[step], rhs_ref[c],
             precision=lax.Precision.HIGHEST, preferred_element_type=jnp.float32,
@@ -269,6 +292,7 @@
 
     for step in range(SUBSTEPS):
         for c in range(comps):
+            prepare(step, c)
             force(step, c)
             if c > 0:
                 finish(step, c - 1)
@@ -290,11 +314,12 @@
         out_shape=jax.ShapeDtypeStruct(velocity.shape, jnp.float32),
         in_specs=[
             pl.BlockSpec(memory_space=pltpu.SMEM),
-            pl.BlockSpec(memory_space=pltpu.VMEM),
-            pl.BlockSpec(memory_space=pltpu.VMEM),
+            pl.BlockSpec(memory_space=pltpu.HBM),
+            pl.BlockSpec(memory_space=pltpu.HBM),
         ],
         out_specs=pl.BlockSpec(memory_space=pltpu.VMEM),
         scratch_shapes=[
+            vmem(*block_inverse.shape),
             vmem(SUBSTEPS, comps, planes, rows + 2 * PAD, lanes),
             vmem(SUBSTEPS, comps, 2, rows, lanes),
             vmem(SUBSTEPS, comps, 2, rows, lanes),
@@ -314,9 +339,10 @@
             pltpu.SemaphoreType.DMA((SUBSTEPS, comps, links)),
             pltpu.SemaphoreType.DMA((links,)),
             pltpu.SemaphoreType.DMA((links,)),
+            pltpu.SemaphoreType.DMA((2,)),
         ],
         compiler_params=pltpu.CompilerParams(
-            collective_id=0, has_side_effects=True, vmem_limit_bytes=40 * 1024 * 1024
+            collective_id=0, has_side_effects=True, vmem_limit_bytes=62 * 1024 * 1024
         ),
     )(stiffness, velocity, block_inverse)
 

time: 53.4 us -> 51.7 us (0.968)
  local copies, waits for them, and re-layouts: 2.94 us -> 1.92 us
  Pallas kernels: 49.6 us -> 49 us
    unnamed x5 -> x1, local copies, waits for them, and re-layouts: 2.94 us -> 1.92 us
    pallas_call x1, Pallas kernels: 49.6 us -> 49 us  [body(): pl.pallas_call(functools.partial(kernel, n_x, n_y), out_shape=jax.ShapeDt...]
where the time goes in v2:
time: 51.7 us; the launch traced here: 51.6 us
  Pallas kernels  49 us (95%)
  local copies, waits for them, and re-layouts  1.92 us (4%)
  between operations  0.66 us (1%)
    pallas_call x1, Pallas kernels, body(): pl.pallas_call(functools.partial(kernel, n_x, n_y), out_shape=jax.ShapeDt...  49 us
    unnamed x1, local copies, waits for them, and re-layouts  1.92 us

profile of v2, /device:TPU:1, one launch (start us, length us, event | category | flops | bytes accessed | tf_op | source)
XLA Modules:
  0.0 51.6 jit_solution(8099193026421231290)
XLA Ops:
  0.7 49.0 %shard_map.37 = f32[3,2,192,128]{3,2,1,0:T(8,128)} custom-call(f32[1]{0:T(128)S(6)} %copy.5.stiff_ref, f32[3,2,192,128]{3,2,1,0:T(8,128)} %vel_ref.1, f32[3,192,192]{2,1,0:T(8,128)} %inv_hbm.1), custom_call_target="tpu_custom_call" | custom-call | tf_op jit(solution)/shard_map/pallas_call | solution.py:312
  49.6 1.9 %copy.6 = f32[3,2,192,128]{3,2,1,0:T(8,128)} copy(f32[3,2,192,128]{3,2,1,0:T(8,128)} %shard_map.37) | data formatting | bytes 1179648
